TPU v7x, 32 devices: a whole 2x2x4 slice. The times are simulated.
32 devices in a mesh: groups: 2 (over y), wide: 8 (over z, x), heads: 2 (over core).
Axes of the slice: x: 2, y: 2, z: 4, core: 2. Of those that a mesh axis runs over, the one named last changes fastest.
Arguments:
- queries: bfloat16 [2048, 2048], P(('groups', 'wide'), 'heads'), parts along dimension 0, may hold values from -160 to 160
- encodings: bfloat16 [1024, 3584], P(('groups', 'wide')), parts along dimension 0, may hold values from -6 to 6
- w_key: bfloat16 [896, 2048], P(None, 'heads'), may hold values from -0.1875 to 0.1875
- w_value: bfloat16 [896, 2048], P(None, 'heads'), may hold values from -0.1875 to 0.1875
- block_owner: int32 [32, 64, 1], P(('groups', 'wide')), parts along dimension 0, may hold values from 0 to 7; in each aligned block of 128 rows (0 to 127, 128 to 255, ..., all dimensions but the last counted through in order) at most 32 rows name the same one
- block_row: int32 [32, 64], P(('groups', 'wide')), parts along dimension 0, may hold values from 0 to 63
Outputs:
- attended: bfloat16 [2048, 2048], P(('groups', 'wide'), 'heads'), parts along dimension 0
There are 2 independent parts, one for each index of `groups`. A program takes and returns all parts, laid end to end along the dimension named above; an argument that names none is the same for every part. Nothing has to cross between parts.
Inputs may be any that keep to these rules, and one draw needn't show every extreme that they name: `block_owner`: within the requests of one index of wide, no owner is named more than 32 times, a bound that some block reaches.
All inputs are finite; a program needn't handle non-finite values.
Results may differ from a plain program's by a relative error of at most 0.0065.
The roundings to bfloat16 on the way count: a program that leaves them out, or rounds other values in their place, can miss the bound.
Values may be sent and summed in bfloat16 or wider, within the bound.
No kernel may reach another device: no remote copies, remote signals or barrier semaphores. Data moves between devices by JAX's collectives and lax.ppermute only.
A program may use at most 64 MiB of HBM per device.

v0:
```python
import jax
import jax.numpy as jnp
from jax import lax
from jax.sharding import PartitionSpec as P

HD = 128
SPAN = 64


def on_device(queries, encodings, w_key, w_value, block_owner, block_row):
    wide_count = lax.axis_size("wide")
    owners = block_owner.reshape(-1)
    stored = block_row.reshape(-1)
    requests = owners.shape[0]
    capacity = 2 * ((requests + wide_count - 1) // wide_count)
    order = jnp.arange(requests, dtype=jnp.int32)
    earlier = (owners[:, None] == owners[None, :]) & (order[None, :] < order[:, None])
    rank = jnp.sum(earlier.astype(jnp.int32), axis=1)
    slot = owners * capacity + rank
    table = jnp.full((wide_count * capacity,), -1, jnp.int32).at[slot].set(stored)
    table = table.reshape(wide_count, capacity)
    asked = lax.all_to_all(table, "wide", split_axis=0, concat_axis=0, tiled=True)
    wanted = jnp.maximum(asked, 0)
    row_width = encodings.shape[1]
    picked = encodings[wanted]
    returned = lax.all_to_all(picked, "wide", split_axis=0, concat_axis=0, tiled=True)
    fetched = returned.reshape(wide_count * capacity, row_width)[slot]
    channels = w_key.shape[0]
    source = fetched.reshape(-1, channels)
    keys = jnp.dot(source, w_key, preferred_element_type=jnp.float32).astype(jnp.bfloat16)
    values = jnp.dot(source, w_value, preferred_element_type=jnp.float32).astype(jnp.bfloat16)
    span_count = queries.shape[0] // SPAN
    heads_local = w_key.shape[1] // HD
    keys = keys.reshape(span_count, -1, heads_local, HD)
    values = values.reshape(span_count, -1, heads_local, HD)
    query_part = queries.reshape(span_count, SPAN, heads_local, HD)
    scores = jnp.einsum(
        "cqhd,ckhd->chqk", query_part, keys, preferred_element_type=jnp.float32
    ) * HD ** (-0.5)
    probs = jax.nn.softmax(scores, axis=-1).astype(jnp.bfloat16)
    mixed = jnp.einsum("chqk,ckhd->cqhd", probs, values, preferred_element_type=jnp.float32)
    return mixed.astype(jnp.bfloat16).reshape(queries.shape)


def solution(mesh):
    placed = (
        P(("groups", "wide"), "heads"),
        P(("groups", "wide"), None),
        P(None, "heads"),
        P(None, "heads"),
        P(("groups", "wide"), None, None),
        P(("groups", "wide"), None),
    )
    return jax.shard_map(
        on_device,
        mesh=mesh,
        in_specs=placed,
        out_specs=P(("groups", "wide"), "heads"),
        check_vma=False,
    )
```

profile of v0, /device:TPU:0, one launch (start us, length us, event | category | flops | bytes accessed | tf_op | source)
XLA Modules:
  0.0 85.8 jit_solution(6737364765455666952)
XLA Ops:
  0.0 0.5 broadcast.69
  0.5 1.4 %fusion.16 = (s32[2,64]{1,0:T(2,128)S(1)}, s32[2,64]{1,0:T(2,128)S(1)}) fusion(s32[2,64,1]{1,2,0:T(1,128)} %param.10, s32[]{:T(128)} %broadcast.69), kind=kLoop, calls=%fused_computation.33 | loop fusion | flops 128 | bytes 1540 | tf_op args[4]
  1.9 0.1 eq.15
  2.0 0.2 convert_reduce_fusion
  2.2 0.8 reshape.97
  3.0 1.0 %scatter_custom_fusion = s32[256]{0:T(256)S(1)} fusion(s32[128]{0:T(128)S(1)} %fusion.12, s32[128]{0:T(128)S(1)} %reshape.97, s32[]{:T(128)} %constant.7.clone.1), kind=kCustom, calls=%fused_computation.31 | custom fusion | bytes 1028 | tf_op jit(solution)/shard_map/scatter | solution.py:20
  4.0 0.1 all_to_all.9
  4.1 13.5 %all_to_all.14 = s32[8,1,32]{2,1,0:T(1,128)S(1)} all-to-all(s32[8,1,32]{2,1,0:T(1,128)S(1)} %all_to_all.9), channel_id=1, replica_groups=mesh['groups'=2,'wide'=8,'heads'=2] {'wide'}, dimensions={0} | all-to-all | bytes 2048 | tf_op jit(solution)/shard_map/all_to_all | solution.py:22
  17.7 5.8 %gather_fusion = bf16[256,3584]{1,0:T(8,128)(2,1)} fusion(bf16[64,3584]{1,0:T(8,128)(2,1)} %param.7, s32[1024]{0:T(1024)S(1)} %pad_clamp_fusion.1), kind=kCustom, calls=%fused_computation | custom fusion | bytes 3671040 | tf_op jit(solution)/shard_map/gather | solution.py:25
  23.5 4.4 %all-to-all-start.1 = ((bf16[8,32,3584]{2,1,0:T(8,128)(2,1)}), bf16[8,32,3584]{2,1,0:T(8,128)(2,1)}, u32[]{:S(2)}, u32[]{:S(2)}) async-start(bf16[8,32,3584]{2,1,0:T(8,128)(2,1)} %bitcast.35), calls=%async_computation.1 | async-start | bytes 3670016 | tf_op jit(solution)/shard_map/all_to_all | solution.py:26
  28.1 41.4 %all-to-all-done.1 = bf16[8,32,3584]{2,1,0:T(8,128)(2,1)} async-done(((bf16[8,32,3584]{2,1,0:T(8,128)(2,1)}), bf16[8,32,3584]{2,1,0:T(8,128)(2,1)}, u32[]{:S(2)}, u32[]{:S(2)}) %all-to-all-start.1) | async-done | bytes 1835040 | tf_op jit(solution)/shard_map/all_to_all | solution.py:26
  69.5 3.8 %gather_fusion.1 = bf16[128,3584]{1,0:T(8,128)(2,1)S(1)} fusion(bf16[256,3584]{1,0:T(8,128)(2,1)} %bitcast.3, s32[1024]{0:T(1024)S(1)} %pad_clamp_fusion), kind=kCustom, calls=%fused_computation.1 | custom fusion | bytes 1835520 | tf_op jit(solution)/shard_map/gather | solution.py:27
  73.2 1.5 %reshape.72 = bf16[512,896]{1,0:T(8,128)(2,1)} reshape(bf16[128,3584]{1,0:T(8,128)(2,1)S(1)} %gather_fusion.1) | data formatting | bytes 1835008 | tf_op jit(solution)/shard_map/reshape | solution.py:29
  74.7 2.4 %fusion.3 = bf16[64,8,8,128]{3,1,2,0:T(8,128)(2,1)S(1)} fusion(bf16[512,896]{1,0:T(8,128)(2,1)} %reshape.72, bf16[896,1024]{1,0:T(8,128)(2,1)S(1)} %copy-done), kind=kOutput, calls=%fused_computation.8 | convolution fusion | flops 940048384 | bytes 3801088 | tf_op jit(solution)/shard_map/dot_general | solution.py:30
  77.1 0.3 copy.18
  77.4 0.5 fusion.5
  77.9 0.3 fusion.17
  78.3 0.3 copy-done.1
  78.6 0.6 copy-done.3
  79.2 1.2 %fusion.2 = bf16[64,8,8,128]{3,1,2,0:T(8,128)(2,1)S(1)} fusion(bf16[512,896]{1,0:T(8,128)(2,1)S(1)} %copy-done.1, bf16[896,1024]{1,0:T(8,128)(2,1)S(1)} %copy-done.3), kind=kOutput, calls=%fused_computation.7 | convolution fusion | flops 940048384 | bytes 3801088 | tf_op jit(solution)/shard_map/dot_general | solution.py:31
  80.5 1.3 %copy.20 = bf16[64,8,8,128]{3,2,1,0:T(8,128)(2,1)} copy(bf16[64,8,8,128]{3,1,2,0:T(8,128)(2,1)S(1)} %fusion.2) | data formatting | bytes 2097152
  81.7 3.1 %fusion.6 = bf16[2,64,8,128]{3,1,2,0:T(8,128)(2,1)S(1)} fusion(bf16[2,256,8,128]{3,2,1,0:T(8,128)(2,1)} %bitcast.38, f32[2,8,64]{2,1,0:T(8,128)S(1)} %fusion.17, f32[2,8,64,256]{3,2,1,0:T(8,128)S(1)} %fusion.5), kind=kOutput, calls=%fused_computation.13 | convolution fusion | flops 68027648 | bytes 2363392 | tf_op jit(solution)/shard_map/chqk,ckhd->cqhd/dot_general | solution.py:41
  84.8 0.2 copy.17
  85.0 0.8 copy.29
  (13 shorter events, 0.3 us)
Async XLA Ops:
  0.0 74.7 %copy-start = (bf16[896,1024]{1,0:T(8,128)(2,1)S(1)}, bf16[896,1024]{1,0:T(8,128)(2,1)}, u32[]{:S(2)}) copy-start(bf16[896,1024]{1,0:T(8,128)(2,1)} %param.8) | copy-start | bytes 5505028
  23.5 4.4 %copy-start.2 = (bf16[128,1024]{1,0:T(8,128)(2,1)S(1)}, bf16[128,1024]{1,0:T(8,128)(2,1)}, u32[]{:S(2)}) copy-start(bf16[128,1024]{1,0:T(8,128)(2,1)} %param.6) | copy-start | bytes 786436
  23.5 45.9 %all-to-all-start.1 = ((bf16[8,32,3584]{2,1,0:T(8,128)(2,1)}), bf16[8,32,3584]{2,1,0:T(8,128)(2,1)}, u32[]{:S(2)}, u32[]{:S(2)}) async-start(bf16[8,32,3584]{2,1,0:T(8,128)(2,1)} %bitcast.35), calls=%async_computation.1 | async-start | bytes 3670016 | tf_op jit(solution)/shard_map/all_to_all | solution.py:26
  77.4 1.2 %copy-start.1 = (bf16[512,896]{1,0:T(8,128)(2,1)S(1)}, bf16[512,896]{1,0:T(8,128)(2,1)}, u32[]{:S(2)}) copy-start(bf16[512,896]{1,0:T(8,128)(2,1)} %reshape.72) | copy-start | bytes 2752516
  77.4 1.8 %copy-start.3 = (bf16[896,1024]{1,0:T(8,128)(2,1)S(1)}, bf16[896,1024]{1,0:T(8,128)(2,1)}, u32[]{:S(2)}) copy-start(bf16[896,1024]{1,0:T(8,128)(2,1)} %param.9) | copy-start | bytes 5505028
where the time goes:
time: 86.2 us; the launch traced here: 85.8 us
  waiting for transfers between devices  41.4 us (48%)
  local copies, waits for them, and re-layouts  17.1 us (20%)
  blocking collectives  13.5 us (16%)
  matrix products  7.24 us (8%)
  starting transfers between devices  4.44 us (5%)
  other arithmetic  1.93 us (2%)
    all_to_all x1, waiting for transfers between devices, on_device(): lax.all_to_all(picked, 'wide', split_axis=0, concat_axis=0, tiled=True)  41.4 us
    all_to_all x1, blocking collectives, on_device(): lax.all_to_all(table, 'wide', split_axis=0, concat_axis=0, tiled=True)  13.5 us
    gather x1, local copies, waits for them, and re-layouts, on_device(): picked = encodings[wanted]  5.84 us
    all_to_all x1, starting transfers between devices, on_device(): lax.all_to_all(picked, 'wide', split_axis=0, concat_axis=0, tiled=True)  4.44 us
    unnamed x13, local copies, waits for them, and re-layouts  3.79 us
    gather x1, local copies, waits for them, and re-layouts, on_device(): fetched = returned.reshape(wide_count * capacity, row_width)[slot]  3.76 us
    dot_general x1, matrix products, on_device(): jnp.einsum('chqk,ckhd->cqhd', probs, values, preferred_element_type=jnp.f...  3.08 us
    dot_general x1, matrix products, on_device(): jnp.dot(source, w_key, preferred_element_type=jnp.float32)  2.43 us
  transfers between devices with their start and end apart: 1, of which 1 were waited for; matrix products, arithmetic and copies ran while one was open for 0% of the time, Pallas kernels for 0%

commit v1 on v0

--- a/solution.py
+++ b/solution.py
@@ -7,12 +7,9 @@
 SPAN = 64
 
 
-def on_device(queries, encodings, w_key, w_value, block_owner, block_row):
+def exchange(encodings, owners, stored, capacity):
     wide_count = lax.axis_size("wide")
-    owners = block_owner.reshape(-1)
-    stored = block_row.reshape(-1)
     requests = owners.shape[0]
-    capacity = 2 * ((requests + wide_count - 1) // wide_count)
     order = jnp.arange(requests, dtype=jnp.int32)
     earlier = (owners[:, None] == owners[None, :]) & (order[None, :] < order[:, None])
     rank = jnp.sum(earlier.astype(jnp.int32), axis=1)
@@ -21,10 +18,29 @@
     table = table.reshape(wide_count, capacity)
     asked = lax.all_to_all(table, "wide", split_axis=0, concat_axis=0, tiled=True)
     wanted = jnp.maximum(asked, 0)
-    row_width = encodings.shape[1]
     picked = encodings[wanted]
     returned = lax.all_to_all(picked, "wide", split_axis=0, concat_axis=0, tiled=True)
-    fetched = returned.reshape(wide_count * capacity, row_width)[slot]
+    return returned.reshape(wide_count * capacity, encodings.shape[1])[slot]
+
+
+def gather(encodings, owners, stored):
+    rows = encodings.shape[0]
+    part = rows // lax.axis_size("heads")
+    mine = lax.dynamic_slice_in_dim(encodings, lax.axis_index("heads") * part, part, 0)
+    database = lax.all_gather(mine, ("wide", "heads"), axis=0, tiled=True)
+    return database[owners * rows + stored]
+
+
+def on_device(queries, encodings, w_key, w_value, block_owner, block_row):
+    wide_count = lax.axis_size("wide")
+    owners = block_owner.reshape(-1)
+    stored = block_row.reshape(-1)
+    requests = owners.shape[0]
+    capacity = 2 * ((requests + wide_count - 1) // wide_count)
+    if encodings.shape[0] <= 2 * capacity:
+        fetched = gather(encodings, owners, stored)
+    else:
+        fetched = exchange(encodings, owners, stored, capacity)
     channels = w_key.shape[0]
     source = fetched.reshape(-1, channels)
     keys = jnp.dot(source, w_key, preferred_element_type=jnp.float32).astype(jnp.bfloat16)

time: 86.2 us -> 84.1 us (0.976)
  blocking collectives: 13.5 us -> 0 us
  between operations: 0.13 us -> 13.5 us
  waiting for transfers between devices: 41.4 us -> 49 us
  starting transfers between devices: 4.44 us -> 0.01 us
  local copies, waits for them, and re-layouts: 17.1 us -> 13 us
  other arithmetic: 1.93 us -> 1.05 us
    all_gather x0 -> x1, waiting for transfers between devices: none -> 49 us  [gather(): database = lax.all_gather(mine, ('wide', 'heads'), axis=0, tiled=True)]
    all_to_all x1 -> x0, waiting for transfers between devices: 41.4 us -> none  [on_device(): lax.all_to_all(picked, 'wide', split_axis=0, concat_axis=0, tiled=True)]
    all_to_all x1 -> x0, blocking collectives: 13.5 us -> none  [on_device(): lax.all_to_all(table, 'wide', split_axis=0, concat_axis=0, tiled=True)]
    gather x2 -> x1, local copies, waits for them, and re-layouts: 9.6 us -> 4.54 us  [gather(): return database[owners * rows + stored]]
    all_to_all x1 -> x0, starting transfers between devices: 4.44 us -> none  [on_device(): lax.all_to_all(picked, 'wide', split_axis=0, concat_axis=0, tiled=True)]
    dynamic_slice x0 -> x1, local copies, waits for them, and re-layouts: none -> 1.77 us  [gather(): lax.dynamic_slice_in_dim(encodings, lax.axis_index('heads') * part, part, 0)]
    unnamed x1 -> x0, other arithmetic: 1.38 us -> none
    scatter x1 -> x0, local copies, waits for them, and re-layouts: 0.97 us -> none  [on_device(): jnp.full((wide_count * capacity,), -1, jnp.int32).at[slot].set(stored)]
  transfers between devices with their start and end apart: 1 -> 1, of which waited for: 1 -> 1; matrix products, arithmetic and copies ran while one was open for 0% -> 3% of each run, Pallas kernels for 0% -> 0%
where the time goes in v1:
time: 84.1 us; the launch traced here: 83.8 us
  waiting for transfers between devices  49 us (58%)
  between operations  13.5 us (16%)
  local copies, waits for them, and re-layouts  13 us (15%)
  matrix products  7.24 us (9%)
  other arithmetic  1.05 us (1%)
    all_gather x1, waiting for transfers between devices, gather(): database = lax.all_gather(mine, ('wide', 'heads'), axis=0, tiled=True)  49 us
    gather x1, local copies, waits for them, and re-layouts, gather(): return database[owners * rows + stored]  4.54 us
    unnamed x10, local copies, waits for them, and re-layouts  4.22 us
    dot_general x1, matrix products, on_device(): jnp.einsum('chqk,ckhd->cqhd', probs, values, preferred_element_type=jnp.f...  3.08 us
    dot_general x1, matrix products, on_device(): jnp.dot(source, w_key, preferred_element_type=jnp.float32)  2.43 us
    dynamic_slice x1, local copies, waits for them, and re-layouts, gather(): lax.dynamic_slice_in_dim(encodings, lax.axis_index('heads') * part, part, 0)  1.77 us
  transfers between devices with their start and end apart: 1, of which 1 were waited for; matrix products, arithmetic and copies ran while one was open for 3% of the time, Pallas kernels for 0%

profile of v1, /device:TPU:0, one launch (start us, length us, event | category | flops | bytes accessed | tf_op | source)
XLA Modules:
  0.0 83.8 jit_solution(6212257393012970556)
XLA Ops:
  6.5 0.0 all-gather.2.cloned.1.call-start
  6.5 1.8 %constant_dynamic-slice_fusion = bf16[32,3584]{1,0:T(8,128)(2,1)} fusion(bf16[64,3584]{1,0:T(8,128)(2,1)} %param.7, s32[]{:T(128)S(6)} %select_n.13), kind=kLoop, calls=%fused_computation.23 | loop fusion | bytes 458756 | tf_op jit(solution)/shard_map/dynamic_slice | solution.py:29
  8.3 0.0 all-gather.2.cloned.1.call-update
  8.3 0.8 reshape.52
  9.1 0.7 multiply_reduce_fusion
  9.8 0.1 mul.31
  9.9 1.0 %copy.15 = bf16[16,8,8,128]{3,2,1,0:T(8,128)(2,1)S(1)} copy(bf16[16,8,8,128]{3,1,2,0:T(8,128)(2,1)} %bitcast.32) | data formatting | bytes 524288
  10.9 49.0 %all-gather.2.cloned.1.call-done = bf16[512,3584]{1,0:T(8,128)(2,1)} async-done(((bf16[32,3584]{1,0:T(8,128)(2,1)}), bf16[512,3584]{1,0:T(8,128)(2,1)}) %all-gather.2.cloned.1.call-update) | async-done | bytes 3670032 | tf_op jit(solution)/shard_map/all_gather | solution.py:30
  59.9 4.5 %gather_fusion = bf16[128,3584]{1,0:T(8,128)(2,1)S(1)} fusion(bf16[512,3584]{1,0:T(8,128)(2,1)} %all-gather.2.cloned.1.call-done, s32[1024]{0:T(1024)S(1)} %pad_clamp_fusion), kind=kCustom, calls=%fused_computation | custom fusion | bytes 1835520 | tf_op jit(solution)/shard_map/gather | solution.py:31
  64.4 1.5 %reshape.53 = bf16[512,896]{1,0:T(8,128)(2,1)} reshape(bf16[128,3584]{1,0:T(8,128)(2,1)S(1)} %gather_fusion) | data formatting | bytes 1835008 | tf_op jit(solution)/shard_map/reshape | solution.py:45
  65.9 0.0 copy-done
  65.9 2.4 %fusion.3 = bf16[64,8,8,128]{3,1,2,0:T(8,128)(2,1)S(1)} fusion(bf16[512,896]{1,0:T(8,128)(2,1)} %reshape.53, bf16[896,1024]{1,0:T(8,128)(2,1)S(1)} %copy-done), kind=kOutput, calls=%fused_computation.6 | convolution fusion | flops 940048384 | bytes 3801088 | tf_op jit(solution)/shard_map/dot_general | solution.py:46
  68.3 0.3 copy.14
  68.6 0.0 copy-start.1
  68.6 0.0 copy-start.2
  68.6 0.5 fusion.5
  69.1 0.3 fusion.13
  69.5 0.3 copy-done.1
  69.8 0.6 copy-done.2
  70.4 1.2 %fusion.2 = bf16[64,8,8,128]{3,1,2,0:T(8,128)(2,1)S(1)} fusion(bf16[512,896]{1,0:T(8,128)(2,1)S(1)} %copy-done.1, bf16[896,1024]{1,0:T(8,128)(2,1)S(1)} %copy-done.2), kind=kOutput, calls=%fused_computation.5 | convolution fusion | flops 940048384 | bytes 3801088 | tf_op jit(solution)/shard_map/dot_general | solution.py:47
  71.7 1.3 %copy.16 = bf16[64,8,8,128]{3,2,1,0:T(8,128)(2,1)} copy(bf16[64,8,8,128]{3,1,2,0:T(8,128)(2,1)S(1)} %fusion.2) | data formatting | bytes 2097152
  72.9 3.1 %fusion.6 = bf16[2,64,8,128]{3,1,2,0:T(8,128)(2,1)S(1)} fusion(bf16[2,256,8,128]{3,2,1,0:T(8,128)(2,1)} %bitcast.30, f32[2,8,64]{2,1,0:T(8,128)S(1)} %fusion.13, f32[2,8,64,256]{3,2,1,0:T(8,128)S(1)} %fusion.5), kind=kOutput, calls=%fused_computation.11 | convolution fusion | flops 68027648 | bytes 2363392 | tf_op jit(solution)/shard_map/chqk,ckhd->cqhd/dot_general | solution.py:57
  76.0 0.2 copy.13
  76.2 0.8 copy.25
  (3 shorter events, 0.0 us)
Async XLA Ops:
  6.5 59.4 %copy-start = (bf16[896,1024]{1,0:T(8,128)(2,1)S(1)}, bf16[896,1024]{1,0:T(8,128)(2,1)}, u32[]{:S(2)}) copy-start(bf16[896,1024]{1,0:T(8,128)(2,1)} %param.8) | copy-start | bytes 5505028
  6.5 53.3 %all-gather.2.cloned.1.call-start = ((), (), s32[]{:S(2)}) async-start(), calls=%async_computation | async-start | bytes 3899392 | tf_op jit(solution)/shard_map/all_gather | solution.py:30
  68.6 1.2 %copy-start.1 = (bf16[512,896]{1,0:T(8,128)(2,1)S(1)}, bf16[512,896]{1,0:T(8,128)(2,1)}, u32[]{:S(2)}) copy-start(bf16[512,896]{1,0:T(8,128)(2,1)} %reshape.53) | copy-start | bytes 2752516
  68.6 1.8 %copy-start.2 = (bf16[896,1024]{1,0:T(8,128)(2,1)S(1)}, bf16[896,1024]{1,0:T(8,128)(2,1)}, u32[]{:S(2)}) copy-start(bf16[896,1024]{1,0:T(8,128)(2,1)} %param.9) | copy-start | bytes 5505028
Sparse Core Ops, SparseCore 0:
  9.6 50.1 all-gather.1

commit v2 on v0

--- a/solution.py
+++ b/solution.py
@@ -1,18 +1,165 @@
+import functools
+
 import jax
 import jax.numpy as jnp
 from jax import lax
+from jax.experimental import pallas as pl
+from jax.experimental.pallas import tpu as pltpu
 from jax.sharding import PartitionSpec as P
 
 HD = 128
 SPAN = 64
-
-
-def on_device(queries, encodings, w_key, w_value, block_owner, block_row):
-    wide_count = lax.axis_size("wide")
-    owners = block_owner.reshape(-1)
-    stored = block_row.reshape(-1)
+SIDE = 2
+LIMIT = 40 * 1024 * 1024
+VMEM = pl.BlockSpec(memory_space=pltpu.VMEM)
+HBM = pl.BlockSpec(memory_space=pl.ANY)
+
+
+def params():
+    return pltpu.CompilerParams(vmem_limit_bytes=LIMIT)
+
+
+def half_kernel(width, enc_ref, out_ref, sem):
+    column = pl.multiple_of(lax.axis_index("heads") * width, 128)
+    copy = pltpu.make_async_copy(enc_ref.at[:, pl.ds(column, width)], out_ref, sem)
+    copy.start()
+    copy.wait()
+
+
+def half_columns(encodings):
+    rows, columns = encodings.shape
+    width = columns // lax.axis_size("heads")
+    return pl.pallas_call(
+        functools.partial(half_kernel, width),
+        out_shape=jax.ShapeDtypeStruct((rows, width), encodings.dtype),
+        in_specs=[HBM],
+        out_specs=HBM,
+        scratch_shapes=[pltpu.SemaphoreType.DMA],
+        compiler_params=params(),
+    )(encodings)
+
+
+def pick_kernel(chunks, index_ref, *refs):
+    sources, out_ref, held, sems = refs[:chunks], refs[chunks], refs[chunks + 1], refs[chunks + 2]
+    rows = sources[0].shape[0]
+    copies = [
+        pltpu.make_async_copy(ref, held.at[pl.ds(n * rows, rows), :], sems.at[n])
+        for n, ref in enumerate(sources)
+    ]
+    for copy in copies:
+        copy.start()
+    places = lax.broadcasted_iota(jnp.int32, (index_ref.shape[0], chunks * rows), 1)
+    chosen = jnp.where(places == index_ref[...], 1.0, 0.0).astype(jnp.bfloat16)
+    for copy in copies:
+        copy.wait()
+    out_ref[...] = jnp.dot(chosen, held[...], preferred_element_type=jnp.float32).astype(out_ref.dtype)
+
+
+def pick(index, sources):
+    chunks = len(sources)
+    rows, width = sources[0].shape
+    return pl.pallas_call(
+        functools.partial(pick_kernel, chunks),
+        out_shape=jax.ShapeDtypeStruct((index.shape[0], width), sources[0].dtype),
+        in_specs=[VMEM] + [HBM] * chunks,
+        out_specs=VMEM,
+        scratch_shapes=[
+            pltpu.VMEM((chunks * rows, width), sources[0].dtype),
+            pltpu.SemaphoreType.DMA((chunks,)),
+        ],
+        compiler_params=params(),
+    )(index, *sources)
+
+
+def by_span(picked, spans, channels):
+    per = picked.shape[0] // spans
+    parts = []
+    for c in range(spans):
+        for t in range(picked.shape[1] // channels):
+            parts.append(picked[c * per : (c + 1) * per, t * channels : (t + 1) * channels])
+    return jnp.concatenate(parts, axis=0)
+
+
+def project_kernel(spans, picked_ref, wk_ref, wv_ref, keys_ref, values_ref):
+    source = by_span(picked_ref[...], spans, wk_ref.shape[0])
+    keys_ref[...] = jnp.dot(source, wk_ref[...], preferred_element_type=jnp.float32).astype(keys_ref.dtype)
+    values_ref[...] = jnp.dot(source, wv_ref[...], preferred_element_type=jnp.float32).astype(values_ref.dtype)
+
+
+def project(picked, w_key, w_value, spans):
+    rows = picked.size // w_key.shape[0]
+    shape = jax.ShapeDtypeStruct((rows, w_key.shape[1]), picked.dtype)
+    return pl.pallas_call(
+        functools.partial(project_kernel, spans),
+        out_shape=(shape, shape),
+        in_specs=[VMEM] * 3,
+        out_specs=(VMEM, VMEM),
+        compiler_params=params(),
+    )(picked, w_key, w_value)
+
+
+def attend_kernel(spans, picked_ref, wk_ref, wv_ref, keys_ref, values_ref, query_ref, out_ref):
+    source = by_span(picked_ref[...], spans, wk_ref.shape[0])
+    keys_more = jnp.dot(source, wk_ref[...], preferred_element_type=jnp.float32).astype(jnp.bfloat16)
+    values_more = jnp.dot(source, wv_ref[...], preferred_element_type=jnp.float32).astype(jnp.bfloat16)
+    per = keys_more.shape[0] // spans
+    for c in range(spans):
+        keys = jnp.concatenate([keys_ref[c * per : (c + 1) * per, :], keys_more[c * per : (c + 1) * per]], axis=0)
+        values = jnp.concatenate([values_ref[c * per : (c + 1) * per, :], values_more[c * per : (c + 1) * per]], axis=0)
+        for h in range(wk_ref.shape[1] // HD):
+            lanes = slice(h * HD, (h + 1) * HD)
+            query = query_ref[c * SPAN : (c + 1) * SPAN, lanes]
+            scores = lax.dot_general(
+                query, keys[:, lanes], (((1,), (1,)), ((), ())), preferred_element_type=jnp.float32
+            ) * HD ** (-0.5)
+            raised = jnp.exp(scores - jnp.max(scores, axis=-1, keepdims=True))
+            probs = (raised * (1.0 / jnp.sum(raised, axis=-1, keepdims=True))).astype(jnp.bfloat16)
+            mixed = jnp.dot(probs, values[:, lanes], preferred_element_type=jnp.float32)
+            out_ref[c * SPAN : (c + 1) * SPAN, lanes] = mixed.astype(out_ref.dtype)
+
+
+def attend(picked, w_key, w_value, keys, values, queries, spans):
+    return pl.pallas_call(
+        functools.partial(attend_kernel, spans),
+        out_shape=jax.ShapeDtypeStruct(queries.shape, queries.dtype),
+        in_specs=[VMEM] * 6,
+        out_specs=VMEM,
+        compiler_params=params(),
+    )(picked, w_key, w_value, keys, values, queries)
+
+
+def spread(mine):
+    wide_count = lax.axis_size("wide")
+    turns = wide_count // SIDE
+    ring = [(n, (n + SIDE) % wide_count) for n in range(wide_count)]
+    across = [(n, n + 1 if n % SIDE == 0 else n - 1) for n in range(wide_count)]
+    own, crossed = [mine], []
+    for k in range(turns):
+        if k + 1 < turns:
+            own.append(lax.ppermute(own[k], "wide", ring))
+        crossed.append(lax.ppermute(own[k], "wide", across))
+    return own + crossed
+
+
+def gathered_plan(queries, encodings, w_key, w_value, owners, stored):
+    wide_count = lax.axis_size("wide")
+    turns = wide_count // SIDE
+    me = lax.axis_index("wide")
+    spans = queries.shape[0] // SPAN
+    mine = half_columns(encodings)
+    sources = spread(mine)
+    back = (me // SIDE - owners // SIDE) % turns
+    place = jnp.where(owners % SIDE == me % SIDE, back, turns + back)
+    index = (place * encodings.shape[0] + stored)[:, None]
+    picked = pick(index, sources)
+    other = lax.ppermute(picked, "heads", [(0, 1), (1, 0)])
+    keys, values = project(picked, w_key, w_value, spans)
+    return attend(other, w_key, w_value, keys, values, queries, spans)
+
+
+def exchange(encodings, owners, stored, capacity):
+    wide_count = lax.axis_size("wide")
     requests = owners.shape[0]
-    capacity = 2 * ((requests + wide_count - 1) // wide_count)
     order = jnp.arange(requests, dtype=jnp.int32)
     earlier = (owners[:, None] == owners[None, :]) & (order[None, :] < order[:, None])
     rank = jnp.sum(earlier.astype(jnp.int32), axis=1)
@@ -21,10 +168,13 @@
     table = table.reshape(wide_count, capacity)
     asked = lax.all_to_all(table, "wide", split_axis=0, concat_axis=0, tiled=True)
     wanted = jnp.maximum(asked, 0)
-    row_width = encodings.shape[1]
     picked = encodings[wanted]
     returned = lax.all_to_all(picked, "wide", split_axis=0, concat_axis=0, tiled=True)
-    fetched = returned.reshape(wide_count * capacity, row_width)[slot]
+    return returned.reshape(wide_count * capacity, encodings.shape[1])[slot]
+
+
+def exchanged_plan(queries, encodings, w_key, w_value, owners, stored, capacity):
+    fetched = exchange(encodings, owners, stored, capacity)
     channels = w_key.shape[0]
     source = fetched.reshape(-1, channels)
     keys = jnp.dot(source, w_key, preferred_element_type=jnp.float32).astype(jnp.bfloat16)
@@ -40,6 +190,17 @@
     probs = jax.nn.softmax(scores, axis=-1).astype(jnp.bfloat16)
     mixed = jnp.einsum("chqk,ckhd->cqhd", probs, values, preferred_element_type=jnp.float32)
     return mixed.astype(jnp.bfloat16).reshape(queries.shape)
+
+
+def on_device(queries, encodings, w_key, w_value, block_owner, block_row):
+    wide_count = lax.axis_size("wide")
+    owners = block_owner.reshape(-1)
+    stored = block_row.reshape(-1)
+    requests = owners.shape[0]
+    capacity = 2 * ((requests + wide_count - 1) // wide_count)
+    if encodings.shape[0] <= 2 * capacity:
+        return gathered_plan(queries, encodings, w_key, w_value, owners, stored)
+    return exchanged_plan(queries, encodings, w_key, w_value, owners, stored, capacity)
 
 
 def solution(mesh):

time: 86.2 us -> 54.8 us (0.64)
  blocking collectives: 13.5 us -> 0 us
  waiting for transfers between devices: 41.4 us -> 28.2 us
  local copies, waits for them, and re-layouts: 17.1 us -> 4.75 us
  Pallas kernels: 0 us -> 11.5 us
  matrix products: 7.24 us -> 0 us
  starting transfers between devices: 4.44 us -> 7.67 us
    all_to_all x1 -> x0, waiting for transfers between devices: 41.4 us -> none  [on_device(): lax.all_to_all(picked, 'wide', split_axis=0, concat_axis=0, tiled=True)]
    ppermute x0 -> x8, waiting for transfers between devices: none -> 28.2 us  [the longest x3 17.3 us: spread(): own.append(lax.ppermute(own[k], 'wide', ring))]
    all_to_all x1 -> x0, blocking collectives: 13.5 us -> none  [on_device(): lax.all_to_all(table, 'wide', split_axis=0, concat_axis=0, tiled=True)]
    pallas_call x0 -> x4, Pallas kernels: none -> 11.5 us  [the longest x1 6.8 us: attend(): pl.pallas_call(functools.partial(attend_kernel, spans), out_shape=jax.Sha...]
    gather x2 -> x0, local copies, waits for them, and re-layouts: 9.6 us -> none  [the longest x1 5.84 us: on_device(): picked = encodings[wanted]]
    ppermute x0 -> x8, starting transfers between devices: none -> 7.67 us  [the longest x4 4.51 us: spread(): crossed.append(lax.ppermute(own[k], 'wide', across))]
    dot_general x4 -> x0, matrix products: 7.24 us -> none  [the longest x1 3.08 us: on_device(): jnp.einsum('chqk,ckhd->cqhd', probs, values, preferred_element_type=jnp.f...]
    all_to_all x1 -> x0, starting transfers between devices: 4.44 us -> none  [on_device(): lax.all_to_all(picked, 'wide', split_axis=0, concat_axis=0, tiled=True)]
  transfers between devices with their start and end apart: 1 -> 8, of which waited for: 1 -> 6; matrix products, arithmetic and copies ran while one was open for 0% -> 8% of each run, Pallas kernels for 0% -> 2%
where the time goes in v2:
time: 54.8 us; the launch traced here: 54.5 us
  waiting for transfers between devices  28.2 us (51%)
  Pallas kernels  11.5 us (21%)
  starting transfers between devices  7.67 us (14%)
  local copies, waits for them, and re-layouts  4.75 us (9%)
  other arithmetic  2.28 us (4%)
    ppermute x3, waiting for transfers between devices, spread(): own.append(lax.ppermute(own[k], 'wide', ring))  17.3 us
    ppermute x4, waiting for transfers between devices, spread(): crossed.append(lax.ppermute(own[k], 'wide', across))  10.9 us
    pallas_call x1, Pallas kernels, attend(): pl.pallas_call(functools.partial(attend_kernel, spans), out_shape=jax.Sha...  6.8 us
    ppermute x4, starting transfers between devices, spread(): crossed.append(lax.ppermute(own[k], 'wide', across))  4.51 us
    pallas_call x1, Pallas kernels, pick(): pl.pallas_call(functools.partial(pick_kernel, chunks), out_shape=jax.Shap...  3.46 us
    unnamed x9, local copies, waits for them, and re-layouts  3.16 us
    ppermute x3, starting transfers between devices, spread(): own.append(lax.ppermute(own[k], 'wide', ring))  3.08 us
    reshape x1, local copies, waits for them, and re-layouts, on_device(): stored = block_row.reshape(-1)  1.45 us
  transfers between devices with their start and end apart: 8, of which 6 were waited for; matrix products, arithmetic and copies ran while one was open for 8% of the time, Pallas kernels for 2%

profile of v2, /device:TPU:0, one launch (start us, length us, event | category | flops | bytes accessed | tf_op | source)
XLA Modules:
  0.0 54.5 jit_solution(17281741628059299659)
XLA Ops:
  0.0 1.2 %copy-done.2 = bf16[64,3584]{1,0:T(8,128)(2,1)S(1)} copy-done((bf16[64,3584]{1,0:T(8,128)(2,1)S(1)}, bf16[64,3584]{1,0:T(8,128)(2,1)}, u32[]{:S(2)}) %copy-start.2) | copy-done | bytes 458776
  1.2 3.1 %collective-permute-start = (bf16[64,1792]{1,0:T(8,128)(2,1)S(1)}, bf16[64,1792]{1,0:T(8,128)(2,1)S(1)}, u32[]{:S(2)}, u32[]{:S(2)}) collective-permute-start(bf16[64,1792]{1,0:T(8,128)(2,1)S(1)} %shard_map.64.refs_0_), channel_id=1, source_target_pairs={{0,4},{2,6},{4,8},{6,10},{8,12},{10,14},{12,0},{14,2},{1,5},{3,7},... | collective-permute-start | bytes 688136 | tf_op jit(solution)/shard_map/ppermute | solution.py:139
  4.3 7.6 %collective-permute-done.refs_1_ = bf16[64,1792]{1,0:T(8,128)(2,1)S(1)} collective-permute-done((bf16[64,1792]{1,0:T(8,128)(2,1)S(1)}, bf16[64,1792]{1,0:T(8,128)(2,1)S(1)}, u32[]{:S(2)}, u32[]{:S(2)}) %collective-permute-start) | collective-permute-done | bytes 229408 | tf_op jit(solution)/shard_map/ppermute | solution.py:139
  11.9 8.6 %collective-permute-done.1.refs_2_ = bf16[64,1792]{1,0:T(8,128)(2,1)S(1)} collective-permute-done((bf16[64,1792]{1,0:T(8,128)(2,1)S(1)}, bf16[64,1792]{1,0:T(8,128)(2,1)S(1)}, u32[]{:S(2)}, u32[]{:S(2)}) %collective-permute-start.1) | collective-permute-done | bytes 229408 | tf_op jit(solution)/shard_map/ppermute | solution.py:139
  20.5 0.0 collective-permute-start.2
  20.5 1.2 %collective-permute-start.3 = (bf16[64,1792]{1,0:T(8,128)(2,1)S(1)}, bf16[64,1792]{1,0:T(8,128)(2,1)S(1)}, u32[]{:S(2)}, u32[]{:S(2)}) collective-permute-start(bf16[64,1792]{1,0:T(8,128)(2,1)S(1)} %shard_map.64.refs_0_), channel_id=1, source_target_pairs={{0,2},{2,0},{4,6},{6,4},{8,10},{10,8},{12,14},{14,12},{1,3},{3,1},... | collective-permute-start | bytes 688136 | tf_op jit(solution)/shard_map/ppermute | solution.py:140
  21.7 0.5 broadcast.148
  22.3 1.3 %reduce.3 = s32[2,64]{1,0:T(2,128)S(1)} reduce(s32[2,64,1]{1,2,0:T(1,128)} %param.10, s32[]{:T(128)} %broadcast.148), dimensions={2}, to_apply=%param.10.reduce_sub_computation.3 | reduce | bytes 1028 | tf_op args[4]
  23.6 0.1 reshape.161
  23.7 1.4 %reshape.162 = s32[128,1]{1,0:T(8,128)} reshape(s32[2,64]{1,0:T(2,128)} %param.11) | data formatting | bytes 1024 | tf_op jit(solution)/shard_map/reshape | solution.py:198
  25.2 0.8 %collective-permute-start.4 = (bf16[64,1792]{1,0:T(8,128)(2,1)S(1)}, bf16[64,1792]{1,0:T(8,128)(2,1)S(1)}, u32[]{:S(2)}, u32[]{:S(2)}) collective-permute-start(bf16[64,1792]{1,0:T(8,128)(2,1)S(1)} %collective-permute-done.refs_1_), channel_id=1, source_target_pairs={{0,2},{2,0},{4,6},{6,4},{8,10},{10,8},{12,14},{14,12},{1,3},{3,1},... | collective-permute-start | bytes 688136 | tf_op jit(solution)/shard_map/ppermute | solution.py:140
  26.0 1.2 %collective-permute-start.5 = (bf16[64,1792]{1,0:T(8,128)(2,1)S(1)}, bf16[64,1792]{1,0:T(8,128)(2,1)S(1)}, u32[]{:S(2)}, u32[]{:S(2)}) collective-permute-start(bf16[64,1792]{1,0:T(8,128)(2,1)S(1)} %collective-permute-done.1.refs_2_), channel_id=1, source_target_pairs={{0,2},{2,0},{4,6},{6,4},{8,10},{10,8},{12,14},{14,12},{1,3},{3,1},... | collective-permute-start | bytes 688136 | tf_op jit(solution)/shard_map/ppermute | solution.py:140
  27.2 1.1 %collective-permute-done.2.refs_3_ = bf16[64,1792]{1,0:T(8,128)(2,1)S(1)} collective-permute-done((bf16[64,1792]{1,0:T(8,128)(2,1)S(1)}, bf16[64,1792]{1,0:T(8,128)(2,1)S(1)}, u32[]{:S(2)}, u32[]{:S(2)}) %collective-permute-start.2) | collective-permute-done | bytes 229408 | tf_op jit(solution)/shard_map/ppermute | solution.py:139
  28.3 1.2 %collective-permute-start.6 = (bf16[64,1792]{1,0:T(8,128)(2,1)S(1)}, bf16[64,1792]{1,0:T(8,128)(2,1)}, u32[]{:S(2)}, u32[]{:S(2)}) collective-permute-start(bf16[64,1792]{1,0:T(8,128)(2,1)S(1)} %collective-permute-done.2.refs_3_), channel_id=1, source_target_pairs={{0,2},{2,0},{4,6},{6,4},{8,10},{10,8},{12,14},{14,12},{1,3},{3,1},... | collective-permute-start | bytes 688136 | tf_op jit(solution)/shard_map/ppermute | solution.py:140
  29.6 0.9 %fusion.4.index_ref = s32[128,1]{1,0:T(8,128)S(1)} fusion(s32[128,1]{1,0:T(8,128)} %reshape.162, s32[128,1]{1,0:T(8,128)S(1)} %reshape.161, s32[]{:T(128)S(6)} %select_n.59, s32[]{:T(128)S(6)} %select_n.58), kind=kLoop, calls=%fused_computation.13 | loop fusion | flops 4608 | bytes 1544 | tf_op jit(solution)/shard_map/add | solution.py:153
  30.5 3.2 %collective-permute-done.4.refs_5_ = bf16[64,1792]{1,0:T(8,128)(2,1)S(1)} collective-permute-done((bf16[64,1792]{1,0:T(8,128)(2,1)S(1)}, bf16[64,1792]{1,0:T(8,128)(2,1)S(1)}, u32[]{:S(2)}, u32[]{:S(2)}) %collective-permute-start.4) | collective-permute-done | bytes 229408 | tf_op jit(solution)/shard_map/ppermute | solution.py:140
  33.7 4.9 %collective-permute-done.5.refs_6_ = bf16[64,1792]{1,0:T(8,128)(2,1)S(1)} collective-permute-done((bf16[64,1792]{1,0:T(8,128)(2,1)S(1)}, bf16[64,1792]{1,0:T(8,128)(2,1)S(1)}, u32[]{:S(2)}, u32[]{:S(2)}) %collective-permute-start.5) | collective-permute-done | bytes 229408 | tf_op jit(solution)/shard_map/ppermute | solution.py:140
  38.6 2.7 %collective-permute-done.6.refs_7_ = bf16[64,1792]{1,0:T(8,128)(2,1)} collective-permute-done((bf16[64,1792]{1,0:T(8,128)(2,1)S(1)}, bf16[64,1792]{1,0:T(8,128)(2,1)}, u32[]{:S(2)}, u32[]{:S(2)}) %collective-permute-start.6) | collective-permute-done | bytes 229408 | tf_op jit(solution)/shard_map/ppermute | solution.py:140
  41.4 3.5 %shard_map.65.picked_ref = bf16[128,1792]{1,0:T(8,128)(2,1)S(1)} custom-call(s32[128,1]{1,0:T(8,128)S(1)} %fusion.4.index_ref, bf16[64,1792]{1,0:T(8,128)(2,1)S(1)} %shard_map.64.refs_0_, bf16[64,1792]{1,0:T(8,128)(2,1)S(1)} %collective-permute-done.refs_1_, bf16[64,1792]{1,0:T(8,128)(2,1)S(1)} %collective-permute-done.1.refs_2_, ...), custom_call_target="tpu_custom_call" | custom-call | tf_op jit(solution)/shard_map/pallas_call | solution.py:61
  44.8 0.1 collective-permute-start.7
  44.9 0.0 copy-start.1
  44.9 1.5 %copy-done.1 = bf16[896,1024]{1,0:T(8,128)(2,1)S(1)} copy-done((bf16[896,1024]{1,0:T(8,128)(2,1)S(1)}, bf16[896,1024]{1,0:T(8,128)(2,1)}, u32[]{:S(2)}) %copy-start.1) | copy-done | bytes 1835032
  46.4 1.2 %shard_map.66 = (bf16[256,1024]{1,0:T(8,128)(2,1)S(1)}, bf16[256,1024]{1,0:T(8,128)(2,1)S(1)}) custom-call(bf16[128,1792]{1,0:T(8,128)(2,1)S(1)} %shard_map.65.picked_ref, bf16[896,1024]{1,0:T(8,128)(2,1)S(1)} %copy-done, bf16[896,1024]{1,0:T(8,128)(2,1)S(1)} %copy-done.1), custom_call_target="tpu_custom_call" | custom-call | tf_op jit(solution)/shard_map/pallas_call | solution.py:92
  47.7 6.8 %shard_map.67 = bf16[128,1024]{1,0:T(8,128)(2,1)} custom-call(bf16[128,1792]{1,0:T(8,128)(2,1)S(1)} %collective-permute-done.7.picked_ref, bf16[896,1024]{1,0:T(8,128)(2,1)S(1)} %copy-done, bf16[896,1024]{1,0:T(8,128)(2,1)S(1)} %copy-done.1, bf16[256,1024]{1,0:T(8,128)(2,1)S(1)} %get-tuple-element.7.keys_ref, ...), custom_call_target="tpu_custom_call" | custom-call | tf_op jit(solution)/shard_map/pallas_call | solution.py:122
  (9 shorter events, 0.1 us)
Async XLA Ops:
  0.0 44.9 %copy-start = (bf16[896,1024]{1,0:T(8,128)(2,1)S(1)}, bf16[896,1024]{1,0:T(8,128)(2,1)}, u32[]{:S(2)}) copy-start(bf16[896,1024]{1,0:T(8,128)(2,1)} %wk_ref.3) | copy-start | bytes 5505028
  0.0 1.2 %copy-start.2 = (bf16[64,3584]{1,0:T(8,128)(2,1)S(1)}, bf16[64,3584]{1,0:T(8,128)(2,1)}, u32[]{:S(2)}) copy-start(bf16[64,3584]{1,0:T(8,128)(2,1)} %enc_ref.1) | copy-start | bytes 1376260
  1.2 10.7 %collective-permute-start = (bf16[64,1792]{1,0:T(8,128)(2,1)S(1)}, bf16[64,1792]{1,0:T(8,128)(2,1)S(1)}, u32[]{:S(2)}, u32[]{:S(2)}) collective-permute-start(bf16[64,1792]{1,0:T(8,128)(2,1)S(1)} %shard_map.64.refs_0_), channel_id=1, source_target_pairs={{0,4},{2,6},{4,8},{6,10},{8,12},{10,14},{12,0},{14,2},{1,5},{3,7},... | collective-permute-start | bytes 688136 | tf_op jit(solution)/shard_map/ppermute | solution.py:139
  11.9 8.6 %collective-permute-start.1 = (bf16[64,1792]{1,0:T(8,128)(2,1)S(1)}, bf16[64,1792]{1,0:T(8,128)(2,1)S(1)}, u32[]{:S(2)}, u32[]{:S(2)}) collective-permute-start(bf16[64,1792]{1,0:T(8,128)(2,1)S(1)} %collective-permute-done.refs_1_), channel_id=1, source_target_pairs={{0,4},{2,6},{4,8},{6,10},{8,12},{10,14},{12,0},{14,2},{1,5},{3,7},... | collective-permute-start | bytes 688136 | tf_op jit(solution)/shard_map/ppermute | solution.py:139
  20.5 7.8 %collective-permute-start.2 = (bf16[64,1792]{1,0:T(8,128)(2,1)S(1)}, bf16[64,1792]{1,0:T(8,128)(2,1)S(1)}, u32[]{:S(2)}, u32[]{:S(2)}) collective-permute-start(bf16[64,1792]{1,0:T(8,128)(2,1)S(1)} %collective-permute-done.1.refs_2_), channel_id=1, source_target_pairs={{0,4},{2,6},{4,8},{6,10},{8,12},{10,14},{12,0},{14,2},{1,5},{3,7},... | collective-permute-start | bytes 688136 | tf_op jit(solution)/shard_map/ppermute | solution.py:139
  20.5 10.0 %collective-permute-start.3 = (bf16[64,1792]{1,0:T(8,128)(2,1)S(1)}, bf16[64,1792]{1,0:T(8,128)(2,1)S(1)}, u32[]{:S(2)}, u32[]{:S(2)}) collective-permute-start(bf16[64,1792]{1,0:T(8,128)(2,1)S(1)} %shard_map.64.refs_0_), channel_id=1, source_target_pairs={{0,2},{2,0},{4,6},{6,4},{8,10},{10,8},{12,14},{14,12},{1,3},{3,1},... | collective-permute-start | bytes 688136 | tf_op jit(solution)/shard_map/ppermute | solution.py:140
  25.2 8.5 %collective-permute-start.4 = (bf16[64,1792]{1,0:T(8,128)(2,1)S(1)}, bf16[64,1792]{1,0:T(8,128)(2,1)S(1)}, u32[]{:S(2)}, u32[]{:S(2)}) collective-permute-start(bf16[64,1792]{1,0:T(8,128)(2,1)S(1)} %collective-permute-done.refs_1_), channel_id=1, source_target_pairs={{0,2},{2,0},{4,6},{6,4},{8,10},{10,8},{12,14},{14,12},{1,3},{3,1},... | collective-permute-start | bytes 688136 | tf_op jit(solution)/shard_map/ppermute | solution.py:140
  26.0 12.7 %collective-permute-start.5 = (bf16[64,1792]{1,0:T(8,128)(2,1)S(1)}, bf16[64,1792]{1,0:T(8,128)(2,1)S(1)}, u32[]{:S(2)}, u32[]{:S(2)}) collective-permute-start(bf16[64,1792]{1,0:T(8,128)(2,1)S(1)} %collective-permute-done.1.refs_2_), channel_id=1, source_target_pairs={{0,2},{2,0},{4,6},{6,4},{8,10},{10,8},{12,14},{14,12},{1,3},{3,1},... | collective-permute-start | bytes 688136 | tf_op jit(solution)/shard_map/ppermute | solution.py:140
  28.3 13.1 %collective-permute-start.6 = (bf16[64,1792]{1,0:T(8,128)(2,1)S(1)}, bf16[64,1792]{1,0:T(8,128)(2,1)}, u32[]{:S(2)}, u32[]{:S(2)}) collective-permute-start(bf16[64,1792]{1,0:T(8,128)(2,1)S(1)} %collective-permute-done.2.refs_3_), channel_id=1, source_target_pairs={{0,2},{2,0},{4,6},{6,4},{8,10},{10,8},{12,14},{14,12},{1,3},{3,1},... | collective-permute-start | bytes 688136 | tf_op jit(solution)/shard_map/ppermute | solution.py:140
  44.8 2.8 %collective-permute-start.7 = (bf16[128,1792]{1,0:T(8,128)(2,1)S(1)}, bf16[128,1792]{1,0:T(8,128)(2,1)S(1)}, u32[]{:S(2)}, u32[]{:S(2)}) collective-permute-start(bf16[128,1792]{1,0:T(8,128)(2,1)S(1)} %shard_map.65.picked_ref), channel_id=1, source_target_pairs={{0,1},{1,0},{2,3},{3,2},{4,5},{5,4},{6,7},{7,6},{8,9},{9,8},{10,11... | collective-permute-start | bytes 1376264 | tf_op jit(solution)/shard_map/ppermute | solution.py:155
  44.9 1.5 %copy-start.1 = (bf16[896,1024]{1,0:T(8,128)(2,1)S(1)}, bf16[896,1024]{1,0:T(8,128)(2,1)}, u32[]{:S(2)}) copy-start(bf16[896,1024]{1,0:T(8,128)(2,1)} %wv_ref.3) | copy-start | bytes 5505028
  46.4 1.3 %copy-start.3 = (bf16[128,1024]{1,0:T(8,128)(2,1)S(1)}, bf16[128,1024]{1,0:T(8,128)(2,1)}, u32[]{:S(2)}) copy-start(bf16[128,1024]{1,0:T(8,128)(2,1)} %query_ref.1) | copy-start | bytes 786436
